TPU v7x, 32 devices: a whole 2x2x4 slice. The times are simulated.
32 devices in a mesh: groups: 2 (over y), rows: 16 (over z, x, core).
Axes of the slice: x: 2, y: 2, z: 4, core: 2. Of those that a mesh axis runs over, the one named last changes fastest.
Arguments:
- latent: bfloat16 [64, 256, 512], P(('groups', 'rows')), parts along dimension 0, may hold values from -100 to 100
- gain_in: float32 [512], replicated, may hold values from 0.1 to 1.9
- shift_in: float32 [512], replicated, may hold values from -3 to 3
- conv_in: bfloat16 [4608, 256], replicated, may hold values from -0.09375 to 0.09375
- gain_mid: float32 [256], replicated, may hold values from 0.1 to 1.9
- shift_mid: float32 [256], replicated, may hold values from -3 to 3
- conv_mid: bfloat16 [2304, 256], replicated, may hold values from -0.125 to 0.125
- skip_weight: bfloat16 [512, 256], replicated, may hold values from -0.25 to 0.25
Outputs:
- decoded: bfloat16 [128, 512, 256], P(('groups', 'rows')), parts along dimension 0
There are 2 independent parts, one for each index of `groups`. A program takes and returns all parts, laid end to end along the dimension named above; an argument that names none is the same for every part. Nothing has to cross between parts.
All inputs are finite; a program needn't handle non-finite values.
Results may differ from a plain program's by a relative error of at most 0.009.
Values may be sent and summed in bfloat16 or wider, within the bound.
A program may use at most 64 MiB of HBM per device.

v0:
```python
import jax
import jax.numpy as jnp
from jax import lax
from jax.sharding import PartitionSpec as P

GROUPS = 32


def padded_2(cells, sides, width):
    for axis, dim in sides:
        count = lax.axis_size(axis)
        ends = count - 1
        head = lax.slice_in_dim(cells, 0, width, axis=dim)
        tail = lax.slice_in_dim(cells, cells.shape[dim] - width, cells.shape[dim], axis=dim)
        cells = jnp.concatenate(
            [
                lax.ppermute(tail, axis, [(i, (i + 1) % count) for i in range(ends)]),
                cells,
                lax.ppermute(head, axis, [((i + 1) % count, i) for i in range(ends)]),
            ],
            axis=dim,
        )
    return cells


def upsample(values):
    return jnp.repeat(jnp.repeat(values, 2, axis=0), 2, axis=1)


def pad_columns(values):
    return jnp.pad(values, ((0, 0), (1, 1), (0, 0)))


def normalize(values, gain, shift):
    height, breadth, chans = values.shape
    width_group = chans // GROUPS
    grouped = values.reshape(height * breadth, GROUPS, width_group)
    count = float(height * breadth * width_group * lax.axis_size("rows"))
    summed, squared = lax.psum(
        (jnp.sum(grouped, axis=(0, 2)), jnp.sum(grouped * grouped, axis=(0, 2))), "rows"
    )
    center = summed / count
    spread = squared / count - center * center
    deviate = grouped - center[None, :, None]
    normed = deviate / jnp.sqrt(spread[None, :, None] + 1e-06)
    return jax.nn.silu(normed.reshape(height, breadth, chans) * gain + shift)


def convolve(padded, weight):
    height = padded.shape[0] - 2
    breadth = padded.shape[1] - 2
    chans = padded.shape[2]
    accum = jnp.zeros((height * breadth, weight.shape[1]), jnp.float32)
    for offset_index in range(9):
        shift_row = offset_index // 3
        shift_col = offset_index % 3
        window = padded[shift_row : shift_row + height, shift_col : shift_col + breadth].reshape(
            -1, chans
        )
        accum = accum + jnp.dot(
            window,
            weight[offset_index * chans : (offset_index + 1) * chans],
            preferred_element_type=jnp.float32,
        )
    return accum.reshape(height, breadth, -1)


def body(latent, gain_in, shift_in, conv_in, gain_mid, shift_mid, conv_mid, skip_weight):
    act = normalize(latent.astype(jnp.float32), gain_in, shift_in).astype(jnp.bfloat16)
    tall = padded_2(upsample(act), (("rows", 0),), 1)
    padded = pad_columns(tall)
    upsampled = tall[1:-1]
    out_rows, out_cols, in_chans = upsampled.shape
    flat_up = upsampled.reshape(-1, in_chans)
    hidden = convolve(padded, conv_in).astype(jnp.bfloat16)
    middle = normalize(hidden.astype(jnp.float32), gain_mid, shift_mid).astype(jnp.bfloat16)
    mid_padded = pad_columns(padded_2(middle, (("rows", 0),), 1))
    second = convolve(mid_padded, conv_mid)
    skipped = jnp.dot(flat_up, skip_weight, preferred_element_type=jnp.float32)
    total_out = second + skipped.reshape(out_rows, out_cols, -1)
    return total_out.astype(jnp.bfloat16)


def solution(mesh):
    placed = (P(("groups", "rows"), None, None), P(), P(), P(), P(), P(), P(), P())
    return jax.shard_map(
        body,
        mesh=mesh,
        in_specs=placed,
        out_specs=P(("groups", "rows"), None, None),
        check_vma=False,
    )
```

profile of v0, /device:TPU:1, one launch (start us, length us, event | category | flops | bytes accessed | tf_op | source)
XLA Modules:
  0.0 117.0 jit_solution(15183971117016011453)
XLA Ops:
  0.0 1.3 %convert_reduce_fusion = (f32[512]{0:T(512)S(1)}, f32[512]{0:T(512)S(1)}) fusion(bf16[2,256,512]{2,1,0:T(8,128)(2,1)} %param.8), kind=kLoop, calls=%fused_computation.38 | loop fusion | flops 1047552 | bytes 528384 | tf_op jit(solution)/shard_map/reduce_sum | solution.py:40
  1.7 30.6 %all-reduce.3 = (f32[32]{0:T(128)S(1)}, f32[32]{0:T(128)S(1)}) all-reduce(f32[32]{0:T(128)S(1)} %reduce_sum.54, f32[32]{0:T(128)S(1)} %reduce_sum.51), channel_id=1, replica_groups=mesh['groups'=2,'rows'=16] {'rows'}, use_global_device_ids=true, to_apply=%region_5.6 | all-reduce | flops 64 | bytes 512 | tf_op jit(solution)/shard_map/psum | solution.py:39
  32.5 1.4 %multiply_convert_fusion.3 = bf16[2,256,512]{2,1,0:T(8,128)(2,1)S(1)} fusion(bf16[2,256,512]{2,1,0:T(8,128)(2,1)} %param.8, f32[512]{0:T(512)} %param.10, f32[512]{0:T(512)} %param.9, f32[512]{0:T(512)S(1)} %div.57, f32[512]{0:T(512)S(1)} %sub.38), kind=kLoop, calls=%fused_computation.50 | loop fusion | flops 2621440 | bytes 1056768 | tf_op jit(solution)/shard_map/convert_element_type | solution.py:69
  34.4 1.0 broadcast_in_dim.24
  35.4 3.0 %collective-permute-start = (bf16[1,512,512]{2,1,0:T(8,128)(2,1)}, bf16[1,512,512]{2,1,0:T(8,128)(2,1)S(1)}, u32[]{:S(2)}, u32[]{:S(2)}) collective-permute-start(bf16[1,512,512]{2,1,0:T(8,128)(2,1)} %broadcast_in_dim.24), channel_id=1, source_target_pairs={{0,1},{1,2},{2,3},{3,4},{4,5},{5,6},{6,7},{7,8},{8,9},{9,10},{10,1... | collective-permute-start | bytes 1572872 | tf_op jit(solution)/shard_map/ppermute | solution.py:17
  38.6 1.0 broadcast_in_dim.27
  39.6 4.6 %collective-permute-start.1 = (bf16[1,512,512]{2,1,0:T(8,128)(2,1)}, bf16[1,512,512]{2,1,0:T(8,128)(2,1)S(1)}, u32[]{:S(2)}, u32[]{:S(2)}) collective-permute-start(bf16[1,512,512]{2,1,0:T(8,128)(2,1)} %broadcast_in_dim.27), channel_id=1, source_target_pairs={{1,0},{2,1},{3,2},{4,3},{5,4},{6,5},{7,6},{8,7},{9,8},{10,9},{11,1... | collective-permute-start | bytes 1572872 | tf_op jit(solution)/shard_map/ppermute | solution.py:19
  44.3 2.4 %broadcast_in_dim.25 = bf16[4,256,2,512]{3,2,1,0:T(2,128)(2,1)} broadcast(bf16[4,256,512]{2,1,0:T(8,128)(2,1)S(1)} %bitcast.55), dimensions={0,1,3} | broadcast | bytes 3145728 | tf_op jit(solution)/shard_map/broadcast_in_dim | solution.py:27
  46.7 2.7 %reshape.106 = bf16[4,512,512]{2,1,0:T(8,128)(2,1)S(1)} reshape(bf16[4,256,2,512]{3,2,1,0:T(2,128)(2,1)} %broadcast_in_dim.25) | data formatting | bytes 4194304 | tf_op jit(solution)/shard_map/reshape | solution.py:27
  49.5 4.1 %reshape.111 = bf16[2048,512]{1,0:T(8,128)(2,1)} reshape(bf16[4,256,2,512]{3,2,1,0:T(2,128)(2,1)} %broadcast_in_dim.25) | data formatting | bytes 4194304 | tf_op jit(solution)/shard_map/reshape | solution.py:57
  53.6 2.3 %fusion.36 = f32[2048,256]{1,0:T(8,128)S(1)} fusion(bf16[2048,512]{1,0:T(8,128)(2,1)} %reshape.111, bf16[4608,256]{1,0:T(8,128)(2,1)} %param.11), kind=kOutput, calls=%fused_computation.62 | convolution fusion | flops 536870912 | bytes 4456448 | tf_op jit(solution)/shard_map/dot_general | solution.py:60
  55.9 1.0 fusion.5
  57.0 2.0 %fusion.59 = (bf16[4,512,512]{2,1,0:T(8,128)(2,1)S(1)}, bf16[4,512,512]{2,1,0:T(8,128)(2,1)S(1)}, bf16[4,512,512]{2,1,0:T(8,128)(2,1)S(1)}, bf16[4,512,512]{2,1,...) fusion(bf16[6,514,512]{2,1,0:T(8,128)(2,1)S(1)} %fusion.5), kind=kLoop, calls=%fused_computation.89 | loop fusion | bytes 25165824 | tf_op jit(solution)/shard_map/slice | solution.py:57
  59.0 0.7 fusion.29
  59.7 0.7 fusion.33
  60.4 0.7 fusion.38
  61.1 0.7 fusion.40
  61.9 0.7 fusion.44
  62.9 0.7 fusion.31
  63.7 0.7 fusion.42
  64.4 2.8 %fusion.58 = (f32[256]{0:T(256)S(1)}, f32[256]{0:T(256)S(1)}, f32[2048,256]{1,0:T(8,128)}) fusion(f32[2048,256]{1,0:T(8,128)S(1)} %fusion.29, f32[2048,256]{1,0:T(8,128)S(1)} %fusion.31, f32[2048,256]{1,0:T(8,128)S(1)} %fusion.33, bf16[2048,512]{1,0:T(8,128)(2,1)S(1)} %bitcast.52, bf16[4608,256]{1,0:T(8,128)(2,1)S(1)} %copy-done.2, ...), kind=kOutput, calls=%fused_computation.88 | convolution fusion | flops 543686144 | bytes 21235712 | tf_op jit(solution)/shard_map/dot_general | solution.py:60
  67.6 28.2 %all-reduce.2 = (f32[32]{0:T(128)S(1)}, f32[32]{0:T(128)S(1)}) all-reduce(f32[32]{0:T(128)S(1)} %reduce_sum.75, f32[32]{0:T(128)S(1)} %reduce_sum.72), channel_id=1, replica_groups=mesh['groups'=2,'rows'=16] {'rows'}, use_global_device_ids=true, to_apply=%region_11.12 | all-reduce | flops 64 | bytes 512 | tf_op jit(solution)/shard_map/psum | solution.py:39
  96.2 2.3 %multiply_convert_fusion.1 = bf16[4,512,256]{2,1,0:T(8,128)(2,1)S(1)} fusion(f32[4,512,256]{2,1,0:T(8,128)} %bitcast.53, f32[256]{0:T(256)S(1)} %copy-done.4, f32[256]{0:T(256)S(1)} %copy-done.5, f32[256]{0:T(256)S(1)} %div.64, f32[256]{0:T(256)S(1)} %sub.43), kind=kLoop, calls=%fused_computation.29 | loop fusion | flops 4718592 | bytes 3149824 | tf_op jit(solution)/shard_map/convert_element_type | solution.py:76
  98.5 1.9 %collective-permute-start.2 = (bf16[1,512,256]{2,1,0:T(8,128)(2,1)S(1)}, bf16[1,512,256]{2,1,0:T(8,128)(2,1)S(1)}, u32[]{:S(2)}, u32[]{:S(2)}) collective-permute-start(bf16[1,512,256]{2,1,0:T(8,128)(2,1)S(1)} %get-tuple-element.29), channel_id=1, source_target_pairs={{0,1},{1,2},{2,3},{3,4},{4,5},{5,6},{6,7},{7,8},{8,9},{9,10},{10,1... | collective-permute-start | bytes 786440 | tf_op jit(solution)/shard_map/ppermute | solution.py:17
  100.4 3.3 %collective-permute-start.3 = (bf16[1,512,256]{2,1,0:T(8,128)(2,1)S(1)}, bf16[1,512,256]{2,1,0:T(8,128)(2,1)S(1)}, u32[]{:S(2)}, u32[]{:S(2)}) collective-permute-start(bf16[1,512,256]{2,1,0:T(8,128)(2,1)S(1)} %get-tuple-element.30), channel_id=1, source_target_pairs={{1,0},{2,1},{3,2},{4,3},{5,4},{6,5},{7,6},{8,7},{9,8},{10,9},{11,1... | collective-permute-start | bytes 786440 | tf_op jit(solution)/shard_map/ppermute | solution.py:19
  103.7 0.7 fusion.27
  104.4 2.1 %collective-permute-done.2 = bf16[1,512,256]{2,1,0:T(8,128)(2,1)S(1)} collective-permute-done((bf16[1,512,256]{2,1,0:T(8,128)(2,1)S(1)}, bf16[1,512,256]{2,1,0:T(8,128)(2,1)S(1)}, u32[]{:S(2)}, u32[]{:S(2)}) %collective-permute-start.2) | collective-permute-done | bytes 262176 | tf_op jit(solution)/shard_map/ppermute | solution.py:17
  106.5 1.6 %collective-permute-done.3 = bf16[1,512,256]{2,1,0:T(8,128)(2,1)S(1)} collective-permute-done((bf16[1,512,256]{2,1,0:T(8,128)(2,1)S(1)}, bf16[1,512,256]{2,1,0:T(8,128)(2,1)S(1)}, u32[]{:S(2)}, u32[]{:S(2)}) %collective-permute-start.3) | collective-permute-done | bytes 262176 | tf_op jit(solution)/shard_map/ppermute | solution.py:19
  108.5 0.8 fusion.60
  111.7 1.1 copy-done.1
  112.8 0.9 convolution_add_fusion.4
  115.7 1.3 %add_convert_fusion = bf16[4,512,256]{2,1,0:T(8,128)(2,1)} fusion(f32[4,512,256]{2,1,0:T(8,128)S(1)} %bitcast.51, f32[4,512,256]{2,1,0:T(8,128)S(1)} %fusion.27), kind=kLoop, calls=%fused_computation.27 | loop fusion | flops 1048576 | bytes 5242880 | tf_op jit(solution)/shard_map/convert_element_type | solution.py:81
  (47 shorter events, 7.2 us)
Async XLA Ops:
  0.0 103.7 %copy-start = (bf16[512,256]{1,0:T(8,128)(2,1)S(1)}, bf16[512,256]{1,0:T(8,128)(2,1)}, u32[]{:S(2)}) copy-start(bf16[512,256]{1,0:T(8,128)(2,1)} %param.15) | copy-start | bytes 786436
  35.4 20.5 %collective-permute-start = (bf16[1,512,512]{2,1,0:T(8,128)(2,1)}, bf16[1,512,512]{2,1,0:T(8,128)(2,1)S(1)}, u32[]{:S(2)}, u32[]{:S(2)}) collective-permute-start(bf16[1,512,512]{2,1,0:T(8,128)(2,1)} %broadcast_in_dim.24), channel_id=1, source_target_pairs={{0,1},{1,2},{2,3},{3,4},{4,5},{5,6},{6,7},{7,8},{8,9},{9,10},{10,1... | collective-permute-start | bytes 1572872 | tf_op jit(solution)/shard_map/ppermute | solution.py:17
  39.6 16.3 %collective-permute-start.1 = (bf16[1,512,512]{2,1,0:T(8,128)(2,1)}, bf16[1,512,512]{2,1,0:T(8,128)(2,1)S(1)}, u32[]{:S(2)}, u32[]{:S(2)}) collective-permute-start(bf16[1,512,512]{2,1,0:T(8,128)(2,1)} %broadcast_in_dim.27), channel_id=1, source_target_pairs={{1,0},{2,1},{3,2},{4,3},{5,4},{6,5},{7,6},{8,7},{9,8},{10,9},{11,1... | collective-permute-start | bytes 1572872 | tf_op jit(solution)/shard_map/ppermute | solution.py:19
  56.9 2.0 %copy-start.2 = (bf16[4608,256]{1,0:T(8,128)(2,1)S(1)}, bf16[4608,256]{1,0:T(8,128)(2,1)}, u32[]{:S(2)}) copy-start(bf16[4608,256]{1,0:T(8,128)(2,1)} %param.11) | copy-start | bytes 7077892
  64.4 31.8 %copy-start.4 = (f32[256]{0:T(256)S(1)}, f32[256]{0:T(256)}, u32[]{:S(2)}) copy-start(f32[256]{0:T(256)} %param.13) | copy-start | bytes 3076
  64.4 31.8 %copy-start.5 = (f32[256]{0:T(256)S(1)}, f32[256]{0:T(256)}, u32[]{:S(2)}) copy-start(f32[256]{0:T(256)} %param.12) | copy-start | bytes 3076
  98.5 8.0 %collective-permute-start.2 = (bf16[1,512,256]{2,1,0:T(8,128)(2,1)S(1)}, bf16[1,512,256]{2,1,0:T(8,128)(2,1)S(1)}, u32[]{:S(2)}, u32[]{:S(2)}) collective-permute-start(bf16[1,512,256]{2,1,0:T(8,128)(2,1)S(1)} %get-tuple-element.29), channel_id=1, source_target_pairs={{0,1},{1,2},{2,3},{3,4},{4,5},{5,6},{6,7},{7,8},{8,9},{9,10},{10,1... | collective-permute-start | bytes 786440 | tf_op jit(solution)/shard_map/ppermute | solution.py:17
  100.4 7.7 %collective-permute-start.3 = (bf16[1,512,256]{2,1,0:T(8,128)(2,1)S(1)}, bf16[1,512,256]{2,1,0:T(8,128)(2,1)S(1)}, u32[]{:S(2)}, u32[]{:S(2)}) collective-permute-start(bf16[1,512,256]{2,1,0:T(8,128)(2,1)S(1)} %get-tuple-element.30), channel_id=1, source_target_pairs={{1,0},{2,1},{3,2},{4,3},{5,4},{6,5},{7,6},{8,7},{9,8},{10,9},{11,1... | collective-permute-start | bytes 786440 | tf_op jit(solution)/shard_map/ppermute | solution.py:19
  108.5 1.3 %copy-start.3 = (bf16[2304,256]{1,0:T(8,128)(2,1)S(1)}, bf16[2304,256]{1,0:T(8,128)(2,1)}, u32[]{:S(2)}) copy-start(bf16[2304,256]{1,0:T(8,128)(2,1)} %param.14) | copy-start | bytes 3538948
  111.2 1.6 %copy-start.1 = (f32[2048,256]{1,0:T(8,128)S(1)}, f32[2048,256]{1,0:T(8,128)}, u32[]{:S(2)}) copy-start(f32[2048,256]{1,0:T(8,128)} %get-tuple-element.37) | copy-start | bytes 6291460
where the time goes:
time: 117 us
  blocking collectives  58.8 us (50%)
  local copies, waits for them, and re-layouts  17.4 us (15%)
  matrix products  15.3 us (13%)
  starting transfers between devices  12.8 us (11%)
  other arithmetic  8.68 us (7%)
  waiting for transfers between devices  3.64 us (3%)
    psum x2, blocking collectives, normalize(): lax.psum((jnp.sum(grouped, axis=(0, 2)), jnp.sum(grouped * grouped, axis=...  58.8 us
    dot_general x18, matrix products, convolve(): jnp.dot(window, weight[offset_index * chans:(offset_index + 1) * chans],...  14.6 us
    ppermute x2, starting transfers between devices, padded_2(): lax.ppermute(head, axis, [((i + 1) % count, i) for i in range(ends)])  7.96 us
    broadcast_in_dim x6, local copies, waits for them, and re-layouts, upsample(): return jnp.repeat(jnp.repeat(values, 2, axis=0), 2, axis=1)  5.04 us
    ppermute x2, starting transfers between devices, padded_2(): lax.ppermute(tail, axis, [(i, (i + 1) % count) for i in range(ends)])  4.89 us
    reshape x1, local copies, waits for them, and re-layouts, convolve(): padded[shift_row:shift_row + height, shift_col:shift_col + breadth]  4.13 us
    slice x2, local copies, waits for them, and re-layouts, convolve(): padded[shift_row:shift_row + height, shift_col:shift_col + breadth]  2.84 us
    reshape x1, local copies, waits for them, and re-layouts, upsample(): return jnp.repeat(jnp.repeat(values, 2, axis=0), 2, axis=1)  2.75 us
  transfers between devices with their start and end apart: 4, of which 2 were waited for; matrix products, arithmetic and copies ran while one was open for 12% of the time, Pallas kernels for 0%

commit v1 on v0

v1 whole, which is shorter than its diff:
```python
import functools

import jax
import jax.numpy as jnp
from jax import lax
from jax.experimental import pallas as pl
from jax.experimental.pallas import tpu as pltpu
from jax.sharding import PartitionSpec as P

GROUPS = 32
EPS = 1e-06
MESH = pl.DeviceIdType.MESH
F32 = jnp.float32
BF16 = jnp.bfloat16

TAP_ORDER = (0, 2, 6, 8, 1, 7, 3, 5, 4)


def dot(a, b):
    return jnp.dot(a, b, preferred_element_type=F32)


def group_total(x, width):
    lane = lax.broadcasted_iota(jnp.int32, x.shape, 1)
    step = 1
    while step < width:
        up = pltpu.roll(x, 128 - step, 1)
        down = pltpu.roll(x, step, 1)
        x = x + jnp.where((lane & step) == 0, up, down)
        step *= 2
    return x


def flat_row(x):
    return jnp.concatenate([x[k : k + 1] for k in range(x.shape[0])], axis=1)


def half_affine(total, width, count, gain, shift):
    rows = gain.shape[1] // 128
    total = group_total(total, width)
    mean = total[0:rows] / count
    var = jnp.maximum(total[rows : 2 * rows] / count - mean * mean, 0.0)
    inv = flat_row(lax.rsqrt(var + EPS))
    mean = flat_row(mean)
    scale = gain * inv
    return 0.5 * scale, 0.5 * (shift - mean * scale)


def silu_of_half(u):
    return u + u * jnp.tanh(u)


def kernel(
    n,
    latent,
    gain_in,
    shift_in,
    conv_in,
    gain_mid,
    shift_mid,
    conv_mid,
    skip_w,
    out,
    xraw,
    xcat,
    w1,
    w2,
    ws,
    de,
    be,
    df,
    bf,
    hid,
    mid,
    skip,
    inter,
    stage,
    stat,
    slots1,
    slots2,
    local_sem,
    halo_send,
    halo_recv,
    stat_send,
    stat_recv,
    out_sem,
):
    me = lax.axis_index("rows")
    width = latent.shape[1]
    chans = latent.shape[2]
    pad = xcat.shape[1]
    outs = out.shape[2]
    first = me == 0
    last = me == n - 1

    load_x = pltpu.make_async_copy(latent, xraw.at[pl.ds(1, 2)], local_sem.at[0])
    load_x.start()
    barrier = pltpu.get_barrier_semaphore()

    def greet(d, carry):
        pl.semaphore_signal(
            barrier, inc=1, device_id={"rows": lax.rem(me + d, n)}, device_id_type=MESH
        )
        return carry

    lax.fori_loop(1, n, greet, 0)
    loads = []
    for slot, tap in enumerate(TAP_ORDER):
        loads.append(
            pltpu.make_async_copy(
                conv_in.at[pl.ds(tap * chans, chans)],
                w1.at[pl.ds(slot * chans, chans)],
                local_sem.at[1 + slot],
            )
        )
    load_w2 = pltpu.make_async_copy(conv_mid, w2, local_sem.at[10])
    load_ws = pltpu.make_async_copy(skip_w, ws, local_sem.at[11])
    for c in loads + [load_ws, load_w2]:
        c.start()

    def peer_copy(slots, index, d):
        return pltpu.make_async_remote_copy(
            src_ref=stat.at[index],
            dst_ref=slots.at[d - 1],
            send_sem=stat_send.at[index, d - 1],
            recv_sem=stat_recv.at[index, d - 1],
            device_id={"rows": lax.rem(me + d, n)},
            device_id_type=MESH,
        )

    def exchange(slots, index):
        def send(d, carry):
            peer_copy(slots, index, d).start()
            return carry

        lax.fori_loop(1, n, send, 0)

    def gathered(slots, index):
        def receive(d, carry):
            peer_copy(slots, index, d).wait_recv()
            return carry

        lax.fori_loop(1, n, receive, 0)
        return stat[index] + jnp.sum(slots[...], axis=0)

    load_x.wait()
    x = xraw[1:3].reshape(2 * width, chans).astype(F32)
    total = jnp.sum(x, axis=0, keepdims=True)
    square = jnp.sum(x * x, axis=0, keepdims=True)
    lanes = chans // 128
    for k in range(lanes):
        stat[0, k : k + 1, :] = total[:, 128 * k : 128 * (k + 1)]
        stat[0, lanes + k : lanes + k + 1, :] = square[:, 128 * k : 128 * (k + 1)]

    pl.semaphore_wait(barrier, n - 1)
    exchange(slots1, 0)
    to_next = pltpu.make_async_remote_copy(
        src_ref=xraw.at[2],
        dst_ref=xraw.at[0],
        send_sem=halo_send.at[0],
        recv_sem=halo_recv.at[0],
        device_id={"rows": lax.rem(me + 1, n)},
        device_id_type=MESH,
    )
    to_prev = pltpu.make_async_remote_copy(
        src_ref=xraw.at[1],
        dst_ref=xraw.at[3],
        send_sem=halo_send.at[1],
        recv_sem=halo_recv.at[1],
        device_id={"rows": lax.rem(me + n - 1, n)},
        device_id_type=MESH,
    )

    @pl.when(jnp.logical_not(last))
    def _():
        to_next.start()

    @pl.when(jnp.logical_not(first))
    def _():
        to_prev.start()

    count1 = float(2 * n * width * (chans // GROUPS))
    scale1, bias1 = half_affine(
        gathered(slots1, 0), chans // GROUPS, count1, gain_in[...], shift_in[...]
    )

    row_in = lax.broadcasted_iota(jnp.int32, (width, chans), 0)
    tail_in = lax.broadcasted_iota(jnp.int32, (8, chans), 0)
    zeros_tail = jnp.zeros((pad - width, chans), BF16)

    def activate(i):
        y = silu_of_half(xraw[i].astype(F32) * scale1 + bias1)
        turned = pltpu.roll(y, 1, 0)
        xcat[i, 0:width, 0:chans] = jnp.where(row_in == 0, 0.0, turned).astype(BF16)
        end = jnp.where(tail_in == 0, turned[0:8], 0.0)
        end = jnp.concatenate([end, jnp.zeros((pad - width - 8, chans), F32)], axis=0)
        xcat[i, width:pad, 0:chans] = end.astype(BF16)
        xcat[i, 0:width, chans:] = y.astype(BF16)
        xcat[i, width:pad, chans:] = zeros_tail

    activate(1)
    activate(2)
    for c in loads:
        c.wait()

    def products(ks, bs):
        pairs = [jnp.concatenate([xcat[k], xcat[k + 1]], axis=1) for k in ks]
        res = dot(jnp.concatenate(pairs, axis=0), w1[0 : 4 * chans])
        for p, k in enumerate(ks):
            de[k] = res[p * pad : (p + 1) * pad]
        pairs = [
            jnp.concatenate([xcat[k, 0:width, chans:], xcat[k + 1, 0:width, chans:]], axis=1)
            for k in ks
        ]
        res = dot(jnp.concatenate(pairs, axis=0), w1[4 * chans : 6 * chans])
        for p, k in enumerate(ks):
            df[k] = res[p * width : (p + 1) * width]
        res = dot(jnp.concatenate([xcat[i] for i in bs], axis=0), w1[6 * chans : 8 * chans])
        for p, i in enumerate(bs):
            be[i] = res[p * pad : (p + 1) * pad]
        res = dot(jnp.concatenate([xcat[i, 0:width, chans:] for i in bs], axis=0), w1[8 * chans : 9 * chans])
        for p, i in enumerate(bs):
            bf[i] = res[p * width : (p + 1) * width]

    sums = [jnp.zeros((8, outs), F32), jnp.zeros((8, outs), F32)]

    def combine(r):
        k, i = r // 2, (r + 1) // 2
        edge = de[k] + be[i]
        whole = df[k] + bf[i]
        even = edge[0:width] + whole
        odd = pltpu.roll(edge, pad - 1, 0)[0:width] + whole
        hid[r, :, 0:outs] = even.astype(BF16)
        hid[r, :, outs:] = odd.astype(BF16)
        if 1 <= r <= 4:
            for v in (even, odd):
                v = v.reshape(width // 8, 8, outs)
                sums[0] = sums[0] + jnp.sum(v, axis=0)
                sums[1] = sums[1] + jnp.sum(v * v, axis=0)

    products((1,), (1, 2))
    combine(2)
    combine(3)

    @pl.when(jnp.logical_not(first))
    def _():
        to_next.wait_recv()
        activate(0)

    @pl.when(first)
    def _():
        xcat[0] = jnp.zeros(xcat.shape[1:], BF16)

    @pl.when(jnp.logical_not(last))
    def _():
        to_prev.wait_recv()
        activate(3)

    @pl.when(last)
    def _():
        xcat[3] = jnp.zeros(xcat.shape[1:], BF16)

    products((0, 2), (0, 3))
    for r in (1, 4, 0, 5):
        combine(r)

    total = jnp.sum(sums[0], axis=0, keepdims=True)
    square = jnp.sum(sums[1], axis=0, keepdims=True)
    lanes = outs // 128
    stat[1] = jnp.zeros(stat.shape[1:], F32)
    for k in range(lanes):
        stat[1, k : k + 1, :] = total[:, 128 * k : 128 * (k + 1)]
        stat[1, lanes + k : lanes + k + 1, :] = square[:, 128 * k : 128 * (k + 1)]
    exchange(slots2, 1)

    load_ws.wait()
    for i in range(2):
        skip[i] = dot(xcat[1 + i, 0:width, chans:], ws[...])
    load_w2.wait()

    count2 = float(8 * n * width * (outs // GROUPS))
    scale2, bias2 = half_affine(
        gathered(slots2, 1), outs // GROUPS, count2, gain_mid[...], shift_mid[...]
    )
    row_mid = lax.broadcasted_iota(jnp.int32, (width, outs), 0)

    def middle(r):
        even = silu_of_half(hid[r, :, 0:outs].astype(F32) * scale2 + bias2)
        odd = silu_of_half(hid[r, :, outs:].astype(F32) * scale2 + bias2)
        if r == 0:
            even = jnp.where(first, 0.0, even)
            odd = jnp.where(first, 0.0, odd)
        if r == 5:
            even = jnp.where(last, 0.0, even)
            odd = jnp.where(last, 0.0, odd)
        before = jnp.where(row_mid == 0, 0.0, pltpu.roll(odd, 1, 0))
        after = jnp.where(row_mid == width - 1, 0.0, pltpu.roll(even, width - 1, 0))
        mid[r, :, 0:outs] = before.astype(BF16)
        mid[r, :, outs : 2 * outs] = even.astype(BF16)
        mid[r, :, 2 * outs : 3 * outs] = odd.astype(BF16)
        mid[r, :, 3 * outs :] = after.astype(BF16)

    def second(pair):
        rows = (2 * pair, 2 * pair + 1)
        base = jnp.concatenate([skip[pair], skip[pair]], axis=0)
        for parity in range(2):
            cols = pl.ds(parity * outs, 3 * outs)
            lhs = jnp.concatenate(
                [
                    jnp.concatenate([mid[r + a, :, cols] for a in range(3)], axis=1)
                    for r in rows
                ],
                axis=0,
            )
            res = dot(lhs, w2[...]) + base
            for h in range(outs // 128):
                inter[pair, h, pl.ds(parity, 2 * width, stride=2), :] = res[
                    :, 128 * h : 128 * (h + 1)
                ]
        for h in range(outs // 128):
            stage[2 * pair : 2 * pair + 2, :, 128 * h : 128 * (h + 1)] = (
                inter[pair, h].astype(BF16).reshape(2, 2 * width, 128)
            )
        pltpu.make_async_copy(
            stage.at[pl.ds(2 * pair, 2)], out.at[pl.ds(2 * pair, 2)], out_sem.at[pair]
        ).start()

    for r in range(4):
        middle(r)
    second(0)
    middle(4)
    middle(5)
    second(1)

    for pair in range(2):
        pltpu.make_async_copy(
            stage.at[pl.ds(2 * pair, 2)], out.at[pl.ds(2 * pair, 2)], out_sem.at[pair]
        ).wait()
    for index, slots in enumerate((slots1, slots2)):

        def sent(d, carry):
            peer_copy(slots, index, d).wait_send()
            return carry

        lax.fori_loop(1, n, sent, 0)

    @pl.when(jnp.logical_not(last))
    def _():
        to_next.wait_send()

    @pl.when(jnp.logical_not(first))
    def _():
        to_prev.wait_send()


def body(n, latent, gain_in, shift_in, conv_in, gain_mid, shift_mid, conv_mid, skip_weight):
    rows, width, chans = latent.shape
    outs = skip_weight.shape[1]
    pad = width + 16
    anywhere = pl.BlockSpec(memory_space=pl.ANY)
    vmem = pl.BlockSpec(memory_space=pltpu.VMEM)
    return pl.pallas_call(
        functools.partial(kernel, n),
        out_shape=jax.ShapeDtypeStruct((2 * rows, 2 * width, outs), BF16),
        in_specs=[anywhere, vmem, vmem, anywhere, vmem, vmem, anywhere, anywhere],
        out_specs=anywhere,
        scratch_shapes=[
            pltpu.VMEM((4, width, chans), BF16),
            pltpu.VMEM((4, pad, 2 * chans), BF16),
            pltpu.VMEM((9 * chans, outs), BF16),
            pltpu.VMEM((9 * outs, outs), BF16),
            pltpu.VMEM((chans, outs), BF16),
            pltpu.VMEM((3, pad, outs), F32),
            pltpu.VMEM((4, pad, outs), F32),
            pltpu.VMEM((3, width, outs), F32),
            pltpu.VMEM((4, width, outs), F32),
            pltpu.VMEM((6, width, 2 * outs), BF16),
            pltpu.VMEM((6, width, 4 * outs), BF16),
            pltpu.VMEM((2, width, outs), F32),
            pltpu.VMEM((2, outs // 128, 4 * width, 128), F32),
            pltpu.VMEM((4, 2 * width, outs), BF16),
            pltpu.VMEM((2, 8, 128), F32),
            pltpu.VMEM((n - 1, 8, 128), F32),
            pltpu.VMEM((n - 1, 8, 128), F32),
            pltpu.SemaphoreType.DMA((12,)),
            pltpu.SemaphoreType.DMA((2,)),
            pltpu.SemaphoreType.DMA((2,)),
            pltpu.SemaphoreType.DMA((2, n - 1)),
            pltpu.SemaphoreType.DMA((2, n - 1)),
            pltpu.SemaphoreType.DMA((2,)),
        ],
        compiler_params=pltpu.CompilerParams(
            collective_id=0, has_side_effects=True, vmem_limit_bytes=56 * 1024 * 1024
        ),
        cost_estimate=pl.CostEstimate(
            flops=4_700_000_000, bytes_accessed=5_400_000, transcendentals=1_300_000
        ),
    )(
        latent,
        gain_in.reshape(1, chans),
        shift_in.reshape(1, chans),
        conv_in,
        gain_mid.reshape(1, outs),
        shift_mid.reshape(1, outs),
        conv_mid,
        skip_weight,
    )


def solution(mesh):
    placed = (P(("groups", "rows"), None, None), P(), P(), P(), P(), P(), P(), P())
    return jax.shard_map(
        functools.partial(body, mesh.shape["rows"]),
        mesh=mesh,
        in_specs=placed,
        out_specs=P(("groups", "rows"), None, None),
        check_vma=False,
    )
```

time: 117 us -> 27.1 us (0.23)
  the two profiles are of different devices: /device:TPU:1 before, /device:TPU:0 now
where the time goes in v1:
time: 27.1 us; the launch traced here: 27 us
  Pallas kernels  24.7 us (91%)
  local copies, waits for them, and re-layouts  2.26 us (8%)
    pallas_call x1, Pallas kernels, body(): pl.pallas_call(functools.partial(kernel, n), out_shape=jax.ShapeDtypeStru...  24.7 us
    unnamed x1, local copies, waits for them, and re-layouts  2.26 us

profile of v1, /device:TPU:0, one launch (start us, length us, event | category | flops | bytes accessed | tf_op | source)
XLA Modules:
  0.0 27.0 jit_solution(14401889359354751697)
XLA Ops:
  0.0 24.7 %shard_map.82 = bf16[4,512,256]{2,1,0:T(8,128)(2,1)} custom-call(bf16[2,256,512]{2,1,0:T(8,128)(2,1)} %latent.1, f32[1,512]{1,0:T(1,128)} %bitcast.4, f32[1,512]{1,0:T(1,128)} %bitcast.5, bf16[4608,256]{1,0:T(8,128)(2,1)} %conv_in.1, f32[1,256]{1,0:T(1,128)} %bitcast.6, f32[1,256]{1,0:T(1,128)} %bitcast.7, bf16[2304,256]{1,0:T(8,128)(2,1)} %conv_mid.1, ...), custom_call_target="tpu_custom_call" | custom-call | flops 4700000256 | bytes 5400000 | tf_op jit(solution)/shard_map/pallas_call | solution.py:362
  24.7 2.3 %copy.10 = bf16[4,512,256]{2,1,0:T(8,128)(2,1)} copy(bf16[4,512,256]{2,1,0:T(8,128)(2,1)} %shard_map.82) | data formatting | bytes 2097152

commit v2 on v1

--- a/solution.py
+++ b/solution.py
@@ -74,7 +74,6 @@
     mid,
     skip,
     inter,
-    stage,
     stat,
     slots1,
     slots2,
@@ -83,7 +82,6 @@
     halo_recv,
     stat_send,
     stat_recv,
-    out_sem,
 ):
     me = lax.axis_index("rows")
     width = latent.shape[1]
@@ -204,23 +202,26 @@
         c.wait()
 
     def products(ks, bs):
-        pairs = [jnp.concatenate([xcat[k], xcat[k + 1]], axis=1) for k in ks]
-        res = dot(jnp.concatenate(pairs, axis=0), w1[0 : 4 * chans])
-        for p, k in enumerate(ks):
-            de[k] = res[p * pad : (p + 1) * pad]
-        pairs = [
-            jnp.concatenate([xcat[k, 0:width, chans:], xcat[k + 1, 0:width, chans:]], axis=1)
-            for k in ks
-        ]
-        res = dot(jnp.concatenate(pairs, axis=0), w1[4 * chans : 6 * chans])
-        for p, k in enumerate(ks):
-            df[k] = res[p * width : (p + 1) * width]
-        res = dot(jnp.concatenate([xcat[i] for i in bs], axis=0), w1[6 * chans : 8 * chans])
-        for p, i in enumerate(bs):
-            be[i] = res[p * pad : (p + 1) * pad]
-        res = dot(jnp.concatenate([xcat[i, 0:width, chans:] for i in bs], axis=0), w1[8 * chans : 9 * chans])
-        for p, i in enumerate(bs):
-            bf[i] = res[p * width : (p + 1) * width]
+        if ks:
+            pairs = [jnp.concatenate([xcat[k], xcat[k + 1]], axis=1) for k in ks]
+            res = dot(jnp.concatenate(pairs, axis=0), w1[0 : 4 * chans])
+            for p, k in enumerate(ks):
+                de[k] = res[p * pad : (p + 1) * pad]
+            pairs = [
+                jnp.concatenate([xcat[k, 0:width, chans:], xcat[k + 1, 0:width, chans:]], axis=1)
+                for k in ks
+            ]
+            res = dot(jnp.concatenate(pairs, axis=0), w1[4 * chans : 6 * chans])
+            for p, k in enumerate(ks):
+                df[k] = res[p * width : (p + 1) * width]
+        if bs:
+            res = dot(jnp.concatenate([xcat[i] for i in bs], axis=0), w1[6 * chans : 8 * chans])
+            for p, i in enumerate(bs):
+                be[i] = res[p * pad : (p + 1) * pad]
+            lhs = jnp.concatenate([xcat[i, 0:width, chans:] for i in bs], axis=0)
+            res = dot(lhs, w1[8 * chans : 9 * chans])
+            for p, i in enumerate(bs):
+                bf[i] = res[p * width : (p + 1) * width]
 
     sums = [jnp.zeros((8, outs), F32), jnp.zeros((8, outs), F32)]
 
@@ -260,8 +261,8 @@
     def _():
         xcat[3] = jnp.zeros(xcat.shape[1:], BF16)
 
-    products((0, 2), (0, 3))
-    for r in (1, 4, 0, 5):
+    products((0, 2), ())
+    for r in (1, 4):
         combine(r)
 
     total = jnp.sum(sums[0], axis=0, keepdims=True)
@@ -273,6 +274,9 @@
         stat[1, lanes + k : lanes + k + 1, :] = square[:, 128 * k : 128 * (k + 1)]
     exchange(slots2, 1)
 
+    products((), (0, 3))
+    for r in (0, 5):
+        combine(r)
     load_ws.wait()
     for i in range(2):
         skip[i] = dot(xcat[1 + i, 0:width, chans:], ws[...])
@@ -318,12 +322,9 @@
                     :, 128 * h : 128 * (h + 1)
                 ]
         for h in range(outs // 128):
-            stage[2 * pair : 2 * pair + 2, :, 128 * h : 128 * (h + 1)] = (
+            out[2 * pair : 2 * pair + 2, :, 128 * h : 128 * (h + 1)] = (
                 inter[pair, h].astype(BF16).reshape(2, 2 * width, 128)
             )
-        pltpu.make_async_copy(
-            stage.at[pl.ds(2 * pair, 2)], out.at[pl.ds(2 * pair, 2)], out_sem.at[pair]
-        ).start()
 
     for r in range(4):
         middle(r)
@@ -332,10 +333,6 @@
     middle(5)
     second(1)
 
-    for pair in range(2):
-        pltpu.make_async_copy(
-            stage.at[pl.ds(2 * pair, 2)], out.at[pl.ds(2 * pair, 2)], out_sem.at[pair]
-        ).wait()
     for index, slots in enumerate((slots1, slots2)):
 
         def sent(d, carry):
@@ -357,13 +354,13 @@
     rows, width, chans = latent.shape
     outs = skip_weight.shape[1]
     pad = width + 16
-    anywhere = pl.BlockSpec(memory_space=pl.ANY)
+    hbm = pl.BlockSpec(memory_space=pltpu.HBM)
     vmem = pl.BlockSpec(memory_space=pltpu.VMEM)
     return pl.pallas_call(
         functools.partial(kernel, n),
-        out_shape=jax.ShapeDtypeStruct((2 * rows, 2 * width, outs), BF16),
-        in_specs=[anywhere, vmem, vmem, anywhere, vmem, vmem, anywhere, anywhere],
-        out_specs=anywhere,
+        out_shape=pltpu.VMEM((2 * rows, 2 * width, outs), BF16),
+        in_specs=[hbm, vmem, vmem, hbm, vmem, vmem, hbm, hbm],
+        out_specs=vmem,
         scratch_shapes=[
             pltpu.VMEM((4, width, chans), BF16),
             pltpu.VMEM((4, pad, 2 * chans), BF16),
@@ -378,7 +375,6 @@
             pltpu.VMEM((6, width, 4 * outs), BF16),
             pltpu.VMEM((2, width, outs), F32),
             pltpu.VMEM((2, outs // 128, 4 * width, 128), F32),
-            pltpu.VMEM((4, 2 * width, outs), BF16),
             pltpu.VMEM((2, 8, 128), F32),
             pltpu.VMEM((n - 1, 8, 128), F32),
             pltpu.VMEM((n - 1, 8, 128), F32),
@@ -387,7 +383,6 @@
             pltpu.SemaphoreType.DMA((2,)),
             pltpu.SemaphoreType.DMA((2, n - 1)),
             pltpu.SemaphoreType.DMA((2, n - 1)),
-            pltpu.SemaphoreType.DMA((2,)),
         ],
         compiler_params=pltpu.CompilerParams(
             collective_id=0, has_side_effects=True, vmem_limit_bytes=56 * 1024 * 1024

time: 27.1 us -> 24.7 us (0.911)
  local copies, waits for them, and re-layouts: 2.26 us -> 0.97 us
  Pallas kernels: 24.7 us -> 23.6 us
    unnamed x1, local copies, waits for them, and re-layouts: 2.26 us -> 0.97 us
    pallas_call x1, Pallas kernels: 24.7 us -> 23.6 us  [body(): pl.pallas_call(functools.partial(kernel, n), out_shape=pltpu.VMEM((2 * ro...]
where the time goes in v2:
time: 24.7 us; the launch traced here: 24.6 us
  Pallas kernels  23.6 us (96%)
  local copies, waits for them, and re-layouts  0.97 us (4%)
    pallas_call x1, Pallas kernels, body(): pl.pallas_call(functools.partial(kernel, n), out_shape=pltpu.VMEM((2 * ro...  23.6 us
    unnamed x1, local copies, waits for them, and re-layouts  0.97 us

profile of v2, /device:TPU:0, one launch (start us, length us, event | category | flops | bytes accessed | tf_op | source)
XLA Modules:
  0.0 24.6 jit_solution(14012023735808310400)
XLA Ops:
  0.0 23.6 %shard_map.82 = bf16[4,512,256]{2,1,0:T(8,128)(2,1)S(1)} custom-call(bf16[2,256,512]{2,1,0:T(8,128)(2,1)} %latent.1, f32[1,512]{1,0:T(1,128)} %bitcast.4, f32[1,512]{1,0:T(1,128)} %bitcast.5, bf16[4608,256]{1,0:T(8,128)(2,1)} %conv_in.1, f32[1,256]{1,0:T(1,128)} %bitcast.6, f32[1,256]{1,0:T(1,128)} %bitcast.7, bf16[2304,256]{1,0:T(8,128)(2,1)} %conv_mid.1, ...), custom_call_target="tpu_custom_call" | custom-call | flops 4700000256 | bytes 5400000 | tf_op jit(solution)/shard_map/pallas_call | solution.py:359
  23.6 1.0 %copy.10 = bf16[4,512,256]{2,1,0:T(8,128)(2,1)} copy(bf16[4,512,256]{2,1,0:T(8,128)(2,1)S(1)} %shard_map.82) | data formatting | bytes 2097152
